TPU v7x, 512 devices: a whole 4x4x16 slice. The times are simulated.
512 devices in a mesh: row: 4 (over x), col: 16 (over z), layer: 8 (over y, core).
Axes of the slice: x: 4, y: 4, z: 16, core: 2. Of those that a mesh axis runs over, the one named last changes fastest.
Arguments:
- a_blocks: bfloat16 [4, 16, 8, 24, 128, 128], P('row', 'col', 'layer'), may hold values from -6 to 6
- a_cells: int32 [4, 16, 8, 24], P('row', 'col', 'layer'), may hold values from 0 to 31, as said below
- a_count: int32 [4, 16, 8], P('row', 'col', 'layer'), may hold values from 12 to 24, as said below
- b_blocks: bfloat16 [4, 16, 8, 80, 128, 128], P('row', 'col', 'layer'), may hold values from -0.0625 to 0.0625
- b_cells: int32 [4, 16, 8, 80], P('row', 'col', 'layer'), may hold values from 0 to 127, as said below
- b_count: int32 [4, 16, 8], P('row', 'col', 'layer'), may hold values from 40 to 80, as said below
- c_cells: int32 [4, 16, 32], P('row', 'col'), may hold values from 0 to 63, as said below
Outputs:
- c_blocks: float32 [4, 16, 32, 128, 128], P('row', 'col', 'layer')
Inputs may be any that keep to these rules, and one draw needn't show every extreme that they name: `a_cells`: positions are distinct within each A panel. `a_count`: some panel is full in every draw. `b_cells`: positions are distinct within each B panel. `b_count`: some panel is full in every draw. `c_cells`: positions are distinct within each tile.
All inputs are finite; a program needn't handle non-finite values.
Results may differ from a plain program's by a relative error of at most 0.0003.
Values may be sent and summed in bfloat16 or wider, within the bound.
A program may use at most 128 MiB of HBM per device.

v0:
```python
import jax
import jax.numpy as jnp
from jax import lax
from jax.sharding import PartitionSpec as P

CR = 4
CC = 16
KW = 8


def shifted(value, axis, by):
    size = lax.axis_size(axis)
    return lax.ppermute(value, axis, [(i, (i + by) % size) for i in range(size)])


def densify(blocks, cell_list, live_count, height, breadth):
    capacity = cell_list.shape[0]
    slot_ids = jnp.arange(capacity, dtype=jnp.int32)
    positions = jnp.arange(height * breadth, dtype=jnp.int32)
    matches = (cell_list[None, :] == positions[:, None]) & (slot_ids[None, :] < live_count)
    slot_index = jnp.sum(jnp.where(matches, slot_ids[None, :], 0), axis=1)
    present = jnp.any(matches, axis=1)
    picked = jnp.take(blocks, slot_index, axis=0)
    picked = jnp.where(present[:, None, None], picked, jnp.zeros((), blocks.dtype))
    return picked.reshape(height, breadth, blocks.shape[1], blocks.shape[2])


def kept_product(left, right, kept_rows, kept_cols):
    left_rows = jnp.take(left, kept_rows, axis=0)
    right_cols = jnp.take(right, kept_cols, axis=1)
    return jnp.einsum("tkxz,ktzy->txy", left_rows, right_cols, preferred_element_type=jnp.float32)


def on_device(a_blocks, a_cells, a_count, b_blocks, b_cells, b_count, c_cells):
    own_left = densify(a_blocks[0, 0, 0], a_cells[0, 0, 0], a_count[0, 0, 0], CR, KW)
    own_right = densify(b_blocks[0, 0, 0], b_cells[0, 0, 0], b_count[0, 0, 0], KW, CC)
    next_left = shifted(own_left, "row", -1)
    next_right = shifted(own_right, "col", -1)
    slot_list = c_cells[0, 0]
    kept_rows = slot_list // CC
    kept_cols = slot_list % CC
    first_stop = kept_product(own_left, own_right, kept_rows, kept_cols)
    both_stops = first_stop + kept_product(next_left, next_right, kept_rows, kept_cols)
    summed = lax.psum_scatter(both_stops, "layer", scatter_dimension=0, tiled=True)
    return summed[None, None]


def solution(mesh):
    return jax.shard_map(
        on_device,
        mesh=mesh,
        in_specs=(
            P("row", "col", "layer", None, None, None),
            P("row", "col", "layer", None),
            P("row", "col", "layer"),
            P("row", "col", "layer", None, None, None),
            P("row", "col", "layer", None),
            P("row", "col", "layer"),
            P("row", "col", None),
        ),
        out_specs=P("row", "col", "layer", None, None),
        check_vma=False,
    )
```

profile of v0, /device:TPU:1, one launch (start us, length us, event | category | flops | bytes accessed | tf_op | source)
XLA Modules:
  0.0 179.7 jit_solution(9117922130417109523)
XLA Ops:
  6.5 0.0 copy-start
  6.5 0.0 reduce-scatter.2.cloned.1.call-start
  7.4 0.8 select_reduce_fusion
  8.1 0.1 reduce_sum.30
  8.2 0.8 fusion.19
  9.0 0.1 broadcast_in_dim.108
  9.1 0.0 copy-done
  9.1 0.0 copy-start.3
  9.1 0.0 copy-start.1
  9.1 3.0 %gather_fusion.1 = bf16[128,128,128]{2,1,0:T(8,128)(2,1)} fusion(bf16[80,128,128]{2,1,0:T(8,128)(2,1)S(1)} %bitcast.52, s32[1024]{0:T(1024)S(1)} %pad_clamp_fusion.1), kind=kCustom, calls=%fused_computation.5 | custom fusion | bytes 8389120 | tf_op jit(solution)/shard_map/jit(_take)/gather | solution.py:23
  12.1 0.0 copy-start.2
  12.1 3.9 %select_select_fusion = bf16[8,16,128,128]{3,2,1,0:T(8,128)(2,1)} fusion(bf16[8,16,128,128]{3,2,1,0:T(8,128)(2,1)} %bitcast.53, pred[8,16]{1,0:T(8,128)(4,1)S(1)} %compare_and_fusion, pred[8,16]{1,0:T(8,128)(4,1)S(1)} %broadcast_in_dim.108), kind=kLoop, calls=%fused_computation.20 | loop fusion | flops 4194304 | bytes 8388864 | tf_op jit(solution)/shard_map/jit(_where)/select_n | solution.py:24
  16.0 11.9 %collective-permute-start.1 = (bf16[8,16,128,128]{3,2,1,0:T(8,128)(2,1)}, bf16[8,16,128,128]{3,2,1,0:T(8,128)(2,1)}, u32[]{:S(2)}, u32[]{:S(2)}) collective-permute-start(bf16[8,16,128,128]{3,2,1,0:T(8,128)(2,1)} %select_select_fusion), channel_id=1, source_target_pairs={{0,120},{8,0},{16,8},{24,16},{32,24},{40,32},{48,40},{56,48},{64,5... | collective-permute-start | bytes 12582920 | tf_op jit(solution)/shard_map/ppermute | solution.py:13
  28.6 0.0 copy-done.3
  28.6 0.1 select_reduce_fusion.1
  28.7 0.1 reduce_sum.27
  28.8 0.1 fusion.21
  28.9 0.1 broadcast_in_dim.101
  29.0 0.0 copy-done.1
  29.0 1.7 gather_fusion
  30.7 2.4 %select_select_fusion.1 = bf16[4,8,128,128]{3,2,1,0:T(8,128)(2,1)} fusion(bf16[4,8,128,128]{3,2,1,0:T(8,128)(2,1)} %bitcast.54, pred[4,8]{1,0:T(4,128)(4,1)S(1)} %compare_and_fusion.3, pred[4,8]{1,0:T(4,128)(4,1)S(1)} %broadcast_in_dim.101), kind=kLoop, calls=%fused_computation.22 | loop fusion | flops 1048576 | bytes 2097216 | tf_op jit(solution)/shard_map/jit(_where)/select_n | solution.py:24
  33.1 4.4 %collective-permute-start = (bf16[4,8,128,128]{3,2,1,0:T(8,128)(2,1)}, bf16[4,8,128,128]{3,2,1,0:T(8,128)(2,1)}, u32[]{:S(2)}, u32[]{:S(2)}) collective-permute-start(bf16[4,8,128,128]{3,2,1,0:T(8,128)(2,1)} %select_select_fusion.1), channel_id=1, source_target_pairs={{0,384},{128,0},{256,128},{384,256},{1,385},{129,1},{257,129},{385... | collective-permute-start | bytes 3145736 | tf_op jit(solution)/shard_map/ppermute | solution.py:13
  37.5 0.0 copy-done.2
  37.6 7.2 %gather_fusion.3 = bf16[32,8,128,128]{3,2,1,0:T(8,128)(2,1)} fusion(bf16[8,16,128,128]{3,2,1,0:T(8,128)(2,1)} %select_select_fusion, s32[1024]{0:T(1024)S(1)} %get-tuple-element.13), kind=kCustom, calls=%fused_computation.1.clone | custom fusion | bytes 16777344 | tf_op jit(solution)/shard_map/jit(_take)/gather | solution.py:30
  44.7 6.2 %gather_fusion.2 = bf16[32,8,128,128]{3,2,1,0:T(8,128)(2,1)} fusion(bf16[4,8,128,128]{3,2,1,0:T(8,128)(2,1)} %select_select_fusion.1, s32[1024]{0:T(1024)S(1)} %get-tuple-element.14), kind=kCustom, calls=%fused_computation.clone | custom fusion | bytes 16777344 | tf_op jit(solution)/shard_map/jit(_take)/gather | solution.py:29
  50.9 9.7 %fusion.2 = f32[32,128,128,1]{2,1,3,0:T(8,128)} fusion(bf16[32,8,128,128]{3,2,1,0:T(8,128)(2,1)} %gather_fusion.3, bf16[32,8,128,128]{3,2,1,0:T(8,128)(2,1)} %gather_fusion.2, pred[32]{0:T(512)(128)(4,1)S(1)} %get-tuple-element.11, pred[32]{0:T(512)(128)(4,1)S(1)} %get-tuple-element.6), kind=kOutput, calls=%fused_computation.8 | convolution fusion | flops 1082130432 | bytes 18874432 | tf_op jit(solution)/shard_map/tkxz,ktzy->txy/dot_general | solution.py:31
  60.6 0.0 collective-permute-done
  60.6 6.2 %gather_fusion.4 = bf16[32,8,128,128]{3,2,1,0:T(8,128)(2,1)} fusion(bf16[4,8,128,128]{3,2,1,0:T(8,128)(2,1)} %collective-permute-done, s32[1024]{0:T(1024)S(1)} %get-tuple-element.14), kind=kCustom, calls=%fused_computation.2.clone | custom fusion | bytes 16777344 | tf_op jit(solution)/shard_map/jit(_take)/gather | solution.py:29
  66.8 50.7 %collective-permute-done.1 = bf16[8,16,128,128]{3,2,1,0:T(8,128)(2,1)} collective-permute-done((bf16[8,16,128,128]{3,2,1,0:T(8,128)(2,1)}, bf16[8,16,128,128]{3,2,1,0:T(8,128)(2,1)}, u32[]{:S(2)}, u32[]{:S(2)}) %collective-permute-start.1) | collective-permute-done | bytes 4194336 | tf_op jit(solution)/shard_map/ppermute | solution.py:13
  117.4 7.2 %gather_fusion.5 = bf16[32,8,128,128]{3,2,1,0:T(8,128)(2,1)} fusion(bf16[8,16,128,128]{3,2,1,0:T(8,128)(2,1)} %collective-permute-done.1, s32[1024]{0:T(1024)S(1)} %get-tuple-element.13), kind=kCustom, calls=%fused_computation.3.clone | custom fusion | bytes 16777344 | tf_op jit(solution)/shard_map/jit(_take)/gather | solution.py:30
  124.6 10.3 %bitcast_add_fusion = f32[32,128,128]{2,1,0:T(8,128)} fusion(f32[32,128,128,1]{2,1,3,0:T(8,128)} %fusion.2, bf16[32,8,128,128]{3,2,1,0:T(8,128)(2,1)} %gather_fusion.5, pred[32]{0:T(512)(128)(4,1)S(1)} %get-tuple-element.11, bf16[32,8,128,128]{3,2,1,0:T(8,128)(2,1)} %gather_fusion.4, pred[32]{0:T(512)(128)(4,1)S(1)} %get-tuple-element.6), kind=kOutput, calls=%fused_computation.21 | convolution fusion | flops 1082654720 | bytes 20971584 | tf_op jit(solution)/shard_map/tkxz,ktzy->txy/dot_general | solution.py:31
  134.9 0.0 reduce-scatter.2.cloned.1.call-update
  134.9 37.9 %reduce-scatter.2.cloned.1.call-done = f32[4,128,128]{2,1,0:T(8,128)} async-done(((f32[32,128,128]{2,1,0:T(8,128)}), f32[4,128,128]{2,1,0:T(8,128)}) %reduce-scatter.2.cloned.1.call-update) | async-done | bytes 262160 | tf_op jit(solution)/shard_map/reduce_scatter | solution.py:44
  (10 shorter events, 0.1 us)
Async XLA Ops:
  6.5 2.5 %copy-start = (bf16[1,1,1,80,128,128]{5,4,3,2,1,0:T(8,128)(2,1)S(1)}, bf16[1,1,1,80,128,128]{5,4,3,2,1,0:T(8,128)(2,1)}, u32[]{:S(2)}) copy-start(bf16[1,1,1,80,128,128]{5,4,3,2,1,0:T(8,128)(2,1)} %param.14) | copy-start | bytes 7864324
  6.5 166.3 %reduce-scatter.2.cloned.1.call-start = ((), (), s32[]{:S(2)}) async-start(), calls=%async_computation.1 | async-start | bytes 2359296 | tf_op jit(solution)/shard_map/reduce_scatter | solution.py:44
  9.1 19.5 %copy-start.3 = (s32[1,1,1,24]{3,2,1,0:T(1,128)S(1)}, s32[1,1,1,24]{3,2,1,0:T(1,128)}, u32[]{:S(2)}) copy-start(s32[1,1,1,24]{3,2,1,0:T(1,128)} %param.12) | copy-start | bytes 292
  9.1 19.9 %copy-start.1 = (bf16[1,1,1,24,128,128]{5,4,3,2,1,0:T(8,128)(2,1)S(1)}, bf16[1,1,1,24,128,128]{5,4,3,2,1,0:T(8,128)(2,1)}, u32[]{:S(2)}) copy-start(bf16[1,1,1,24,128,128]{5,4,3,2,1,0:T(8,128)(2,1)} %param.11) | copy-start | bytes 2359300
  12.1 25.4 %copy-start.2 = (s32[1,1,32]{2,1,0:T(1,128)S(1)}, s32[1,1,32]{2,1,0:T(1,128)}, u32[]{:S(2)}) copy-start(s32[1,1,32]{2,1,0:T(1,128)} %param.17) | copy-start | bytes 388
  16.0 101.5 %collective-permute-start.1 = (bf16[8,16,128,128]{3,2,1,0:T(8,128)(2,1)}, bf16[8,16,128,128]{3,2,1,0:T(8,128)(2,1)}, u32[]{:S(2)}, u32[]{:S(2)}) collective-permute-start(bf16[8,16,128,128]{3,2,1,0:T(8,128)(2,1)} %select_select_fusion), channel_id=1, source_target_pairs={{0,120},{8,0},{16,8},{24,16},{32,24},{40,32},{48,40},{56,48},{64,5... | collective-permute-start | bytes 12582920 | tf_op jit(solution)/shard_map/ppermute | solution.py:13
  33.1 27.4 %collective-permute-start = (bf16[4,8,128,128]{3,2,1,0:T(8,128)(2,1)}, bf16[4,8,128,128]{3,2,1,0:T(8,128)(2,1)}, u32[]{:S(2)}, u32[]{:S(2)}) collective-permute-start(bf16[4,8,128,128]{3,2,1,0:T(8,128)(2,1)} %select_select_fusion.1), channel_id=1, source_target_pairs={{0,384},{128,0},{256,128},{384,256},{1,385},{129,1},{257,129},{385... | collective-permute-start | bytes 3145736 | tf_op jit(solution)/shard_map/ppermute | solution.py:13
Sparse Core Ops, SparseCore 0:
  135.0 37.7 reduce-scatter.1
where the time goes:
time: 181 us; the launch traced here: 180 us
  waiting for transfers between devices  88.6 us (49%)
  local copies, waits for them, and re-layouts  31.8 us (18%)
  matrix products  19.9 us (11%)
  starting transfers between devices  16.3 us (9%)
  between operations  14.9 us (8%)
  other arithmetic  8.04 us (4%)
    ppermute x2, waiting for transfers between devices, shifted(): lax.ppermute(value, axis, [(i, (i + by) % size) for i in range(size)])  50.7 us
    reduce_scatter x1, waiting for transfers between devices, on_device(): lax.psum_scatter(both_stops, 'layer', scatter_dimension=0, tiled=True)  37.9 us
    dot_general x2, matrix products, kept_product(): jnp.einsum('tkxz,ktzy->txy', left_rows, right_cols, preferred_element_typ...  19.9 us
    ppermute x2, starting transfers between devices, shifted(): lax.ppermute(value, axis, [(i, (i + by) % size) for i in range(size)])  16.3 us
    gather x2, local copies, waits for them, and re-layouts, kept_product(): right_cols = jnp.take(right, kept_cols, axis=1)  14.4 us
    gather x2, local copies, waits for them, and re-layouts, kept_product(): left_rows = jnp.take(left, kept_rows, axis=0)  12.3 us
    select_n x2, other arithmetic, densify(): jnp.where(present[:, None, None], picked, jnp.zeros((), blocks.dtype))  6.26 us
    gather x2, local copies, waits for them, and re-layouts, densify(): picked = jnp.take(blocks, slot_index, axis=0)  4.76 us
  transfers between devices with their start and end apart: 3, of which 2 were waited for; matrix products, arithmetic and copies ran while one was open for 19% of the time, Pallas kernels for 0%

commit v1 on v0

v1 whole, which is shorter than its diff:
```python
import jax
import jax.numpy as jnp
from jax import lax
from jax.experimental import pallas as pl
from jax.experimental.pallas import tpu as pltpu
from jax.sharding import PartitionSpec as P

CR = 4
CC = 16
KW = 8
BS = 128
ROWS1 = (32, 32, 32, 32)
ROWS2 = (32, 32, 32, 32)
MESH = pl.DeviceIdType.MESH
CORE, FA, FB, DA, DB, SA, SB, ZZ = range(8)


def plan_units():
    units = []
    for tile, rows in enumerate((ROWS1, ROWS2)):
        start = 0
        for part, height in enumerate(rows):
            units.append((tile, part, start, height))
            start += height
    return units


def plan_steps(first, total):
    steps = []
    for n in range(first + 3):
        if n < first:
            steps.append(("product", n))
        for lag, name in ((1, "chip"), (2, "forward"), (3, "finish")):
            if 0 <= n - lag < first:
                steps.append((name, n - lag))
    for n in range(first, total):
        steps.append(("product", n))
        if n > first:
            steps.append(("finish", n - 1))
        steps.append(("chip", n))
        if n > first:
            steps.append(("home", n - 1))
        steps.append(("forward", n))
    steps.append(("finish", total - 1))
    steps.append(("home", total - 1))
    return steps


def slot_table(cells, count, capacity):
    lanes = lax.broadcasted_iota(jnp.int32, (1, BS), 1)

    def place(s, table):
        cell = jnp.where(s < count, cells[0, 0, 0, s], -1)
        return jnp.where(lanes == cell, s, table)

    return lax.fori_loop(0, capacity, place, jnp.full((1, BS), capacity, jnp.int32), unroll=8)


def kernel(shape, a_cells, a_count, b_cells, b_count, c_cells, a_hbm, b_hbm, out, *scratch):
    n_row, n_col, n_layer = shape
    units = plan_units()
    parts = len(ROWS2)
    a_next = scratch[:parts]
    (a_own, b_slots, left, right, dense, kept, away, core_in,
     fa_in, fb_in, da_in, db_in, sa_in, sb_in, z_in,
     a_table, b_table, c_list, a_table_in, c_list_in,
     a_at, b_at, a_next_at, c_next_at,
     local_sem, a_send, a_recv, int_send, int_recv, send_sem, recv_sem) = scratch[parts:]
    cap_a = a_hbm.shape[3]
    cap_b = b_hbm.shape[3]

    r, c, l = lax.axis_index("row"), lax.axis_index("col"), lax.axis_index("layer")
    ny = n_layer // 2
    y, p = l // 2, l % 2
    r_up, r_down = lax.rem(r + 1, n_row), lax.rem(r + n_row - 1, n_row)
    c_up, c_down = lax.rem(c + 1, n_col), lax.rem(c + n_col - 1, n_col)
    a_to, a_from = (r_down, c_up, l), (r_up, c_down, l)
    sibling = (r, c, y * 2 + 1 - p)
    y_up = (r, c, lax.rem(y + 1, ny) * 2 + p)
    y_down = (r, c, lax.rem(y + ny - 1, ny) * 2 + p)
    z_up, z_down = (r, c_up, l), (r, c_down, l)

    barrier = pltpu.get_barrier_semaphore()
    others = (a_to, a_from, sibling, y_up, y_down, z_up, z_down)
    for other in others:
        pl.semaphore_signal(barrier, inc=1, device_id=other, device_id_type=MESH)

    b_copy = pltpu.make_async_copy(b_hbm.at[0, 0, 0], b_slots.at[pl.ds(0, cap_b)], local_sem.at[0])
    a_copy = pltpu.make_async_copy(a_hbm.at[0, 0, 0], a_own.at[pl.ds(0, cap_a)], local_sem.at[1])
    a_copy.start()
    b_copy.start()
    pl.semaphore_wait(barrier, len(others))

    def remote(src, dst, send, recv, device):
        return pltpu.make_async_remote_copy(
            src_ref=src, dst_ref=dst, send_sem=send, recv_sem=recv, device_id=device, device_id_type=MESH
        )

    a_copies = []
    for tile, part, start, height in units:
        if tile == 1:
            a_copies.append(
                remote(
                    a_hbm.at[0, 0, 0, :, pl.ds(start, height), :],
                    a_next[part].at[pl.ds(0, cap_a)],
                    a_send.at[part],
                    a_recv.at[part],
                    a_to,
                )
            )
    for copy in a_copies:
        copy.start()

    lanes = lax.broadcasted_iota(jnp.int32, (1, BS), 1)

    def list_cell(t, row):
        return jnp.where(lanes == t, c_cells[0, 0, t], row)

    a_table[...] = slot_table(a_cells, a_count[0, 0, 0], cap_a)
    a_at_copy = pltpu.make_async_copy(a_table, a_at, local_sem.at[2])
    a_at_copy.start()
    b_table[...] = slot_table(b_cells, b_count[0, 0, 0], cap_b)
    b_at_copy = pltpu.make_async_copy(b_table, b_at, local_sem.at[3])
    b_at_copy.start()
    a_table_copy = remote(a_table, a_table_in, int_send.at[0], int_recv.at[0], a_to)
    a_table_copy.start()
    c_list[...] = lax.fori_loop(0, c_cells.shape[2], list_cell, jnp.zeros((1, BS), jnp.int32), unroll=8)
    c_list_copy = remote(c_list, c_list_in, int_send.at[1], int_recv.at[1], z_up)
    c_list_copy.start()

    a_own[cap_a] = jnp.zeros((BS, BS), a_own.dtype)
    b_slots[cap_b] = jnp.zeros((BS, BS), b_slots.dtype)
    for tile, part, start, height in units:
        if tile == 1:
            a_next[part][cap_a] = jnp.zeros((height, BS), a_own.dtype)

    b_at_copy.wait()
    b_copy.wait()

    @pl.loop(0, KW)
    def _(k):
        for j in range(CC):
            right[j // 2, pl.ds(k * BS, BS), (j % 2) * BS:(j % 2 + 1) * BS] = b_slots[b_at[0, k * CC + j]]

    a_at_copy.wait()
    a_copy.wait()

    a_next_at_copy = pltpu.make_async_copy(a_table_in, a_next_at, local_sem.at[4])
    c_next_at_copy = pltpu.make_async_copy(c_list_in, c_next_at, local_sem.at[5])

    def copies_of(u):
        tile, part, start, height = units[u]
        rows = pl.ds(start, height)

        def link(kind, src, dst, device):
            return remote(src, dst, send_sem.at[u, kind], recv_sem.at[u, kind], device)

        def blocks(first, count):
            return kept.at[tile, pl.ds(first, count), rows, :]

        links = {
            CORE: link(CORE, away.at[tile, :, rows, :], core_in.at[tile, :, rows, :], sibling),
            FA: link(FA, blocks(8, 2), fa_in.at[tile, :, rows, :], y_up),
            FB: link(FB, blocks(10, 2), fb_in.at[tile, :, rows, :], y_down),
            DB: link(DB, blocks(6, 2), db_in.at[tile, :, rows, :], y_up),
            DA: link(DA, blocks(12, 2), da_in.at[tile, :, rows, :], y_down),
            SA: link(SA, blocks(4, 2), sa_in.at[tile, :, rows, :], y_up),
            SB: link(SB, blocks(14, 2), sb_in.at[tile, :, rows, :], y_down),
        }
        if tile == 1:
            links[ZZ] = link(ZZ, blocks(0, 4), z_in.at[:, rows, :], z_down)
        return links

    copies = [copies_of(u) for u in range(len(units))]

    def product(u):
        tile, part, start, height = units[u]
        rows = pl.ds(start, height)
        if tile == 1:
            if part == 0:
                a_table_copy.wait_recv()
                a_next_at_copy.start()
                c_list_copy.wait_recv()
                c_next_at_copy.start()
                a_next_at_copy.wait()
                c_next_at_copy.wait()
            a_copies[part].wait_recv()
        for i in range(CR):
            for k in range(KW):
                if tile == 0:
                    block = a_own[a_at[0, i * KW + k], rows, :]
                else:
                    block = a_next[part][a_next_at[0, i * KW + k]]
                left[i * height:(i + 1) * height, k * BS:(k + 1) * BS] = block

        @pl.loop(0, CC // 2)
        def _(j):
            total = jnp.dot(left[0:CR * height, :], right[j], preferred_element_type=jnp.float32)
            for i in range(CR):
                for s in range(2):
                    dense[i * CC + 2 * j + s, 0:height, :] = total[i * height:(i + 1) * height, s * BS:(s + 1) * BS]

        @pl.loop(0, ny)
        def _(e):
            base = lax.rem(y + e, ny) * 8
            for q in range(4):
                for ours, target in ((False, away), (True, kept)):
                    t = base + (p if ours else 1 - p) * 4 + q
                    cell = c_cells[0, 0, t] if tile == 0 else c_next_at[0, t]
                    target[tile, e * 4 + q, rows, :] = dense[cell, 0:height, :]

        copies[u][CORE].start()

    def chip(u):
        tile, part, start, height = units[u]
        rows = pl.ds(start, height)
        copies[u][CORE].wait_recv()
        for e, sends in ((2, (FA, FB)), (1, (DB,)), (3, (DA,)), (0, ())):
            span = slice(e * 4, e * 4 + 4)
            kept[tile, span, rows, :] += core_in[tile, span, rows, :]
            for kind in sends:
                copies[u][kind].start()

    def forward(u):
        tile, part, start, height = units[u]
        rows = pl.ds(start, height)
        for came, sent, first, arrived in ((FA, SA, 4, fa_in), (FB, SB, 14, fb_in)):
            copies[u][came].wait_recv()
            kept[tile, first:first + 2, rows, :] += arrived[tile, :, rows, :]
            copies[u][sent].start()

    def finish(u):
        tile, part, start, height = units[u]
        rows = pl.ds(start, height)
        for kind in (DA, DB, SA, SB):
            copies[u][kind].wait_recv()
        upper = kept[tile, 0:2, rows, :] + da_in[tile, :, rows, :] + sa_in[tile, :, rows, :]
        lower = kept[tile, 2:4, rows, :] + db_in[tile, :, rows, :] + sb_in[tile, :, rows, :]
        if tile == 0:
            out[0, 0, 0:2, rows, :] = upper
            out[0, 0, 2:4, rows, :] = lower
        else:
            kept[tile, 0:2, rows, :] = upper
            kept[tile, 2:4, rows, :] = lower
            copies[u][ZZ].start()

    def home(u):
        tile, part, start, height = units[u]
        rows = pl.ds(start, height)
        copies[u][ZZ].wait_recv()
        out[0, 0, :, rows, :] += z_in[:, rows, :]

    stages = {"product": product, "chip": chip, "forward": forward, "finish": finish, "home": home}
    for name, u in plan_steps(len(ROWS1), len(units)):
        stages[name](u)

    for copy in a_copies:
        copy.wait_send()
    a_table_copy.wait_send()
    c_list_copy.wait_send()
    for links in copies:
        for copy in links.values():
            copy.wait_send()


def solution(mesh):
    shape = tuple(mesh.shape[axis] for axis in ("row", "col", "layer"))

    def on_device(a_blocks, a_cells, a_count, b_blocks, b_cells, b_count, c_cells):
        cap_a, cap_b, cap_c = a_blocks.shape[3], b_blocks.shape[3], c_cells.shape[2]
        here = cap_c // shape[2]
        units = len(ROWS1) + len(ROWS2)
        bf16, f32, i32 = jnp.bfloat16, jnp.float32, jnp.int32
        vmem, smem, dma = pltpu.VMEM, pltpu.SMEM, pltpu.SemaphoreType.DMA
        pair = (2, here // 2, BS, BS)
        return pl.pallas_call(
            lambda *refs: kernel(shape, *refs),
            out_shape=jax.ShapeDtypeStruct((1, 1, here, BS, BS), f32),
            in_specs=[pl.BlockSpec(memory_space=pltpu.SMEM)] * 5 + [pl.BlockSpec(memory_space=pl.ANY)] * 2,
            out_specs=pl.BlockSpec(memory_space=pltpu.VMEM),
            scratch_shapes=[vmem((cap_a + 1, height, BS), bf16) for height in ROWS2] + [
                vmem((cap_a + 1, BS, BS), bf16),
                vmem((cap_b + 1, BS, BS), bf16),
                vmem((CR * max(ROWS1 + ROWS2), KW * BS), bf16),
                vmem((CC // 2, KW * BS, 2 * BS), bf16),
                vmem((CR * CC, max(ROWS1 + ROWS2), BS), f32),
                vmem((2, cap_c // 2, BS, BS), f32),
                vmem((2, cap_c // 2, BS, BS), f32),
                vmem((2, cap_c // 2, BS, BS), f32),
                vmem(pair, f32), vmem(pair, f32), vmem(pair, f32), vmem(pair, f32), vmem(pair, f32), vmem(pair, f32),
                vmem((here, BS, BS), f32),
                vmem((1, BS), i32), vmem((1, BS), i32), vmem((1, BS), i32), vmem((1, BS), i32), vmem((1, BS), i32),
                smem((1, BS), i32), smem((1, BS), i32), smem((1, BS), i32), smem((1, BS), i32),
                dma((6,)),
                dma((len(ROWS2),)), dma((len(ROWS2),)),
                dma((2,)), dma((2,)),
                dma((units, 8)), dma((units, 8)),
            ],
            compiler_params=pltpu.CompilerParams(
                collective_id=0, has_side_effects=True, vmem_limit_bytes=56 * 1024 * 1024
            ),
        )(a_cells, a_count, b_cells, b_count, c_cells, a_blocks, b_blocks)

    return jax.shard_map(
        on_device,
        mesh=mesh,
        in_specs=(
            P("row", "col", "layer", None, None, None),
            P("row", "col", "layer", None),
            P("row", "col", "layer"),
            P("row", "col", "layer", None, None, None),
            P("row", "col", "layer", None),
            P("row", "col", "layer"),
            P("row", "col", None),
        ),
        out_specs=P("row", "col", "layer", None, None),
        check_vma=False,
    )
```

time: 181 us -> 71.8 us (0.40)
  waiting for transfers between devices: 88.6 us -> 0 us
  Pallas kernels: 0 us -> 67.4 us
  local copies, waits for them, and re-layouts: 31.8 us -> 1.67 us
  matrix products: 19.9 us -> 0 us
  starting transfers between devices: 16.3 us -> 0 us
  between operations: 14.9 us -> 1.3 us
  other arithmetic: 8.04 us -> 0 us
    pallas_call x0 -> x1, Pallas kernels: none -> 67.4 us  [on_device(): pl.pallas_call(lambda *refs: kernel(shape, *refs), out_shape=jax.ShapeDty...]
    ppermute x2 -> x0, waiting for transfers between devices: 50.7 us -> none  [shifted(): lax.ppermute(value, axis, [(i, (i + by) % size) for i in range(size)])]
    reduce_scatter x1 -> x0, waiting for transfers between devices: 37.9 us -> none  [on_device(): lax.psum_scatter(both_stops, 'layer', scatter_dimension=0, tiled=True)]
    gather x6 -> x0, local copies, waits for them, and re-layouts: 31.5 us -> none  [the longest x2 14.4 us: kept_product(): right_cols = jnp.take(right, kept_cols, axis=1)]
    dot_general x2 -> x0, matrix products: 19.9 us -> none  [kept_product(): jnp.einsum('tkxz,ktzy->txy', left_rows, right_cols, preferred_element_typ...]
    ppermute x2 -> x0, starting transfers between devices: 16.3 us -> none  [shifted(): lax.ppermute(value, axis, [(i, (i + by) % size) for i in range(size)])]
    select_n x4 -> x0, other arithmetic: 6.27 us -> none  [the longest x2 6.26 us: densify(): jnp.where(present[:, None, None], picked, jnp.zeros((), blocks.dtype))]
  transfers between devices with their start and end apart: 3 -> 0, of which waited for: 2 -> 0; matrix products, arithmetic and copies ran while one was open for 19% -> 0% of each run, Pallas kernels for 0% -> 0%
where the time goes in v1:
time: 71.8 us; the launch traced here: 70.4 us
  Pallas kernels  67.4 us (94%)
  local copies, waits for them, and re-layouts  1.67 us (2%)
  between operations  1.3 us (2%)
    pallas_call x1, Pallas kernels, on_device(): pl.pallas_call(lambda *refs: kernel(shape, *refs), out_shape=jax.ShapeDty...  67.4 us
    unnamed x1, local copies, waits for them, and re-layouts  1.67 us

profile of v1, /device:TPU:1, one launch (start us, length us, event | category | flops | bytes accessed | tf_op | source)
XLA Modules:
  0.0 70.4 jit_solution(11437057622281230771)
XLA Ops:
  1.3 67.4 %shard_map.73 = f32[1,1,4,128,128]{4,3,2,1,0:T(8,128)} custom-call(s32[1,1,1,24]{3,2,1,0:T(1,128)} %refs_0_.1, s32[1,1,1]{2,1,0:T(1,128)S(6)} %copy.9.refs_1_, s32[1,1,1,80]{3,2,1,0:T(1,128)} %refs_2_.1, s32[1,1,1]{2,1,0:T(1,128)S(6)} %copy.10.refs_3_, s32[1,1,32]{2,1,0:T(1,128)} %refs_4_.1, bf16[1,1,1,24,128,128]{5,4,3,2,1,0:T(8,128)(2,1)} %refs_5_.1, ...), custom_call_target="tpu_custom_call" | custom-call | tf_op jit(solution)/shard_map/pallas_call | solution.py:276
  68.8 1.7 %copy.11 = f32[1,1,4,128,128]{4,3,2,1,0:T(8,128)} copy(f32[1,1,4,128,128]{4,3,2,1,0:T(8,128)} %shard_map.73) | data formatting | bytes 524288

commit v2 on v1

--- a/solution.py
+++ b/solution.py
@@ -9,8 +9,9 @@
 CC = 16
 KW = 8
 BS = 128
-ROWS1 = (32, 32, 32, 32)
-ROWS2 = (32, 32, 32, 32)
+ROWS1 = (64, 64)
+ROWS2 = (48, 32, 32, 16)
+DIRECT = (5,)
 MESH = pl.DeviceIdType.MESH
 CORE, FA, FB, DA, DB, SA, SB, ZZ = range(8)
 
@@ -25,25 +26,13 @@
     return units
 
 
-def plan_steps(first, total):
-    steps = []
-    for n in range(first + 3):
-        if n < first:
-            steps.append(("product", n))
-        for lag, name in ((1, "chip"), (2, "forward"), (3, "finish")):
-            if 0 <= n - lag < first:
-                steps.append((name, n - lag))
-    for n in range(first, total):
-        steps.append(("product", n))
-        if n > first:
-            steps.append(("finish", n - 1))
-        steps.append(("chip", n))
-        if n > first:
-            steps.append(("home", n - 1))
-        steps.append(("forward", n))
-    steps.append(("finish", total - 1))
-    steps.append(("home", total - 1))
-    return steps
+STEPS = (
+    ("product", 0), ("product", 1), ("chip", 0), ("send", 1), ("chip", 1), ("product", 2), ("send", 2),
+    ("forward", 0), ("forward", 1), ("chip", 2), ("product", 3), ("send", 3), ("finish", 0), ("forward", 2),
+    ("finish", 1), ("chip", 3), ("product", 4), ("forward", 3), ("finish", 2), ("chip", 4), ("product", 5),
+    ("home", 2), ("finish", 3), ("chip", 5), ("forward", 4), ("home", 3), ("finish", 4), ("home", 5),
+    ("home", 4),
+)
 
 
 def slot_table(cells, count, capacity):
@@ -62,7 +51,7 @@
     parts = len(ROWS2)
     a_next = scratch[:parts]
     (a_own, b_slots, left, right, dense, kept, away, core_in,
-     fa_in, fb_in, da_in, db_in, sa_in, sb_in, z_in,
+     fa_in, fb_in, da_in, db_in, sa_in, sb_in, z_in, parts_in,
      a_table, b_table, c_list, a_table_in, c_list_in,
      a_at, b_at, a_next_at, c_next_at,
      local_sem, a_send, a_recv, int_send, int_recv, send_sem, recv_sem) = scratch[parts:]
@@ -78,10 +67,11 @@
     sibling = (r, c, y * 2 + 1 - p)
     y_up = (r, c, lax.rem(y + 1, ny) * 2 + p)
     y_down = (r, c, lax.rem(y + ny - 1, ny) * 2 + p)
-    z_up, z_down = (r, c_up, l), (r, c_down, l)
 
     barrier = pltpu.get_barrier_semaphore()
-    others = (a_to, a_from, sibling, y_up, y_down, z_up, z_down)
+    owners = [(r, c_down, lax.rem(y + e, ny) * 2 + p) for e in range(4)]
+    sources = [(r, c_up, lax.rem(y + ny - e, ny) * 2 + p) for e in range(4)]
+    others = (a_to, a_from, sibling, y_up, y_down, *owners, *sources)
     for other in others:
         pl.semaphore_signal(barrier, inc=1, device_id=other, device_id_type=MESH)
 
@@ -108,8 +98,7 @@
                     a_to,
                 )
             )
-    for copy in a_copies:
-        copy.start()
+    a_copies[0].start()
 
     lanes = lax.broadcasted_iota(jnp.int32, (1, BS), 1)
 
@@ -125,7 +114,7 @@
     a_table_copy = remote(a_table, a_table_in, int_send.at[0], int_recv.at[0], a_to)
     a_table_copy.start()
     c_list[...] = lax.fori_loop(0, c_cells.shape[2], list_cell, jnp.zeros((1, BS), jnp.int32), unroll=8)
-    c_list_copy = remote(c_list, c_list_in, int_send.at[1], int_recv.at[1], z_up)
+    c_list_copy = remote(c_list, c_list_in, int_send.at[1], int_recv.at[1], sources[0])
     c_list_copy.start()
 
     a_own[cap_a] = jnp.zeros((BS, BS), a_own.dtype)
@@ -158,6 +147,14 @@
         def blocks(first, count):
             return kept.at[tile, pl.ds(first, count), rows, :]
 
+        if u in DIRECT:
+            base = start - units[DIRECT[0]][2]
+            links = {
+                1 + e: link(1 + e, blocks(4 * e, 4), parts_in.at[e, :, pl.ds(base, height), :], owners[e])
+                for e in range(4)
+            }
+            links[CORE] = link(CORE, away.at[tile, :, rows, :], core_in.at[tile, :, rows, :], sibling)
+            return links
         links = {
             CORE: link(CORE, away.at[tile, :, rows, :], core_in.at[tile, :, rows, :], sibling),
             FA: link(FA, blocks(8, 2), fa_in.at[tile, :, rows, :], y_up),
@@ -168,7 +165,7 @@
             SB: link(SB, blocks(14, 2), sb_in.at[tile, :, rows, :], y_down),
         }
         if tile == 1:
-            links[ZZ] = link(ZZ, blocks(0, 4), z_in.at[:, rows, :], z_down)
+            links[ZZ] = link(ZZ, blocks(0, 4), z_in.at[:, rows, :], owners[0])
         return links
 
     copies = [copies_of(u) for u in range(len(units))]
@@ -218,7 +215,7 @@
         for e, sends in ((2, (FA, FB)), (1, (DB,)), (3, (DA,)), (0, ())):
             span = slice(e * 4, e * 4 + 4)
             kept[tile, span, rows, :] += core_in[tile, span, rows, :]
-            for kind in sends:
+            for kind in (1 + e,) if u in DIRECT else sends:
                 copies[u][kind].start()
 
     def forward(u):
@@ -247,15 +244,26 @@
     def home(u):
         tile, part, start, height = units[u]
         rows = pl.ds(start, height)
-        copies[u][ZZ].wait_recv()
-        out[0, 0, :, rows, :] += z_in[:, rows, :]
-
-    stages = {"product": product, "chip": chip, "forward": forward, "finish": finish, "home": home}
-    for name, u in plan_steps(len(ROWS1), len(units)):
+        if u in DIRECT:
+            near = pl.ds(start - units[DIRECT[0]][2], height)
+            for e in range(4):
+                copies[u][1 + e].wait_recv()
+            out[0, 0, :, rows, :] += (parts_in[0, :, near, :] + parts_in[1, :, near, :]) + (
+                parts_in[2, :, near, :] + parts_in[3, :, near, :]
+            )
+        else:
+            copies[u][ZZ].wait_recv()
+            out[0, 0, :, rows, :] += z_in[:, rows, :]
+
+    def send(part):
+        a_copies[part - 1].wait_send()
+        a_copies[part].start()
+
+    stages = {"send": send, "product": product, "chip": chip, "forward": forward, "finish": finish, "home": home}
+    for name, u in STEPS:
         stages[name](u)
 
-    for copy in a_copies:
-        copy.wait_send()
+    a_copies[-1].wait_send()
     a_table_copy.wait_send()
     c_list_copy.wait_send()
     for links in copies:
@@ -289,6 +297,7 @@
                 vmem((2, cap_c // 2, BS, BS), f32),
                 vmem(pair, f32), vmem(pair, f32), vmem(pair, f32), vmem(pair, f32), vmem(pair, f32), vmem(pair, f32),
                 vmem((here, BS, BS), f32),
+                vmem((4, here, sum(ROWS2[u - len(ROWS1)] for u in DIRECT), BS), f32),
                 vmem((1, BS), i32), vmem((1, BS), i32), vmem((1, BS), i32), vmem((1, BS), i32), vmem((1, BS), i32),
                 smem((1, BS), i32), smem((1, BS), i32), smem((1, BS), i32), smem((1, BS), i32),
                 dma((6,)),

time: 71.8 us -> 50.6 us (0.70); the launches traced: 70.4 us -> 50.4 us
  Pallas kernels: 67.4 us -> 47.4 us
    pallas_call x1, Pallas kernels: 67.4 us -> 47.4 us  [on_device(): pl.pallas_call(lambda *refs: kernel(shape, *refs), out_shape=jax.ShapeDty...]
where the time goes in v2:
time: 50.6 us; the launch traced here: 50.4 us
  Pallas kernels  47.4 us (94%)
  local copies, waits for them, and re-layouts  1.67 us (3%)
  between operations  1.3 us (3%)
    pallas_call x1, Pallas kernels, on_device(): pl.pallas_call(lambda *refs: kernel(shape, *refs), out_shape=jax.ShapeDty...  47.4 us
    unnamed x1, local copies, waits for them, and re-layouts  1.67 us

profile of v2, /device:TPU:1, one launch (start us, length us, event | category | flops | bytes accessed | tf_op | source)
XLA Modules:
  0.0 50.4 jit_solution(13046338220918565151)
XLA Ops:
  1.3 47.4 %shard_map.73 = f32[1,1,4,128,128]{4,3,2,1,0:T(8,128)} custom-call(s32[1,1,1,24]{3,2,1,0:T(1,128)} %refs_0_.1, s32[1,1,1]{2,1,0:T(1,128)S(6)} %copy.9.refs_1_, s32[1,1,1,80]{3,2,1,0:T(1,128)} %refs_2_.1, s32[1,1,1]{2,1,0:T(1,128)S(6)} %copy.10.refs_3_, s32[1,1,32]{2,1,0:T(1,128)} %refs_4_.1, bf16[1,1,1,24,128,128]{5,4,3,2,1,0:T(8,128)(2,1)} %refs_5_.1, ...), custom_call_target="tpu_custom_call" | custom-call | tf_op jit(solution)/shard_map/pallas_call | solution.py:284
  48.7 1.7 %copy.11 = f32[1,1,4,128,128]{4,3,2,1,0:T(8,128)} copy(f32[1,1,4,128,128]{4,3,2,1,0:T(8,128)} %shard_map.73) | data formatting | bytes 524288

commit v3 on v2

--- a/solution.py
+++ b/solution.py
@@ -190,7 +190,7 @@
                     block = a_next[part][a_next_at[0, i * KW + k]]
                 left[i * height:(i + 1) * height, k * BS:(k + 1) * BS] = block
 
-        @pl.loop(0, CC // 2)
+        @pl.loop(0, CC // 2, unroll=2)
         def _(j):
             total = jnp.dot(left[0:CR * height, :], right[j], preferred_element_type=jnp.float32)
             for i in range(CR):

time: 50.6 us -> 50.1 us (level); the launches traced: 50.4 us -> 49.1 us
  Pallas kernels: 47.4 us -> 46.1 us
    pallas_call x1, Pallas kernels: 47.4 us -> 46.1 us  [on_device(): pl.pallas_call(lambda *refs: kernel(shape, *refs), out_shape=jax.ShapeDty...]
where the time goes in v3:
time: 50.1 us; the launch traced here: 49.1 us
  Pallas kernels  46.1 us (92%)
  local copies, waits for them, and re-layouts  1.67 us (3%)
  between operations  1.3 us (3%)
    pallas_call x1, Pallas kernels, on_device(): pl.pallas_call(lambda *refs: kernel(shape, *refs), out_shape=jax.ShapeDty...  46.1 us
    unnamed x1, local copies, waits for them, and re-layouts  1.67 us

profile of v3, /device:TPU:1, one launch (start us, length us, event | category | flops | bytes accessed | tf_op | source)
XLA Modules:
  0.0 49.1 jit_solution(16450798476818861468)
XLA Ops:
  1.3 46.1 %shard_map.73 = f32[1,1,4,128,128]{4,3,2,1,0:T(8,128)} custom-call(s32[1,1,1,24]{3,2,1,0:T(1,128)} %refs_0_.1, s32[1,1,1]{2,1,0:T(1,128)S(6)} %copy.9.refs_1_, s32[1,1,1,80]{3,2,1,0:T(1,128)} %refs_2_.1, s32[1,1,1]{2,1,0:T(1,128)S(6)} %copy.10.refs_3_, s32[1,1,32]{2,1,0:T(1,128)} %refs_4_.1, bf16[1,1,1,24,128,128]{5,4,3,2,1,0:T(8,128)(2,1)} %refs_5_.1, ...), custom_call_target="tpu_custom_call" | custom-call | tf_op jit(solution)/shard_map/pallas_call | solution.py:284
  47.4 1.7 %copy.11 = f32[1,1,4,128,128]{4,3,2,1,0:T(8,128)} copy(f32[1,1,4,128,128]{4,3,2,1,0:T(8,128)} %shard_map.73) | data formatting | bytes 524288
